TPU v7x, 256 devices: a whole 4x4x8 slice. The times are simulated.
256 devices in a mesh: cfg: 8 (over x, y_lo), seq: 32 (over z, y_hi, core).
Axes of the slice: x: 4, y: 4 (y_hi: 2, y_lo: 2; y = y_hi * 2 + y_lo), z: 8, core: 2. Of those that a mesh axis runs over, the one named last changes fastest.
Arguments:
- latent: float32 [8, 2048, 64], P('cfg', 'seq'), may hold values from -6 to 6
- query_key_value: bfloat16 [8, 4096, 6144], P('cfg', 'seq'), may hold values from -8 to 8
- text_kv: bfloat16 [8, 128, 4096], P('cfg'), may hold values from -12 to 12
- text_len: int32 [8], P('cfg'), may hold values from 1 to 128, as said below
- hidden: bfloat16 [8, 4096, 2048], P('cfg', 'seq'), may hold values from -20 to 20
- modulation: float32 [8, 3, 2048], P('cfg'), may hold values from -3 to 3
- out_weight: bfloat16 [2048, 2048], replicated, may hold values from -6 to 6
- final_weight: bfloat16 [2048, 64], replicated, may hold values from -0.125 to 0.125
- guide_table: float32 [12, 3, 2048], replicated, may hold values from -3 to 3
- time_index: int32 [4], replicated, may hold values from 0 to 49
- guide_index: int32 [4], replicated, may hold values from 0 to 11
Outputs:
- latent_next: float32 [8, 2048, 64], P('cfg', 'seq')
- guided_velocity: float32 [8, 2048, 64], P('cfg', 'seq')
- final_grad: float32 [2048, 64], P(('cfg', 'seq'))
- table_grad: float32 [12, 3, 2048], P(None, None, ('cfg', 'seq'))
Inputs may be any that keep to these rules, and one draw needn't show every extreme that they name: `text_len`: some branch row uses all 128 text tokens.
All inputs are finite; a program needn't handle non-finite values.
Results may differ from a plain program's by a relative error of at most 0.0055.
Values may be sent and summed in bfloat16 or wider, within the bound.
No kernel may reach another device: no remote copies, remote signals or barrier semaphores. Data moves between devices by JAX's collectives and lax.ppermute only.
A program may use at most 64 MiB of HBM per device.

v0:
```python
import functools
import math

import jax
import jax.numpy as jnp
from jax import lax
from jax.experimental import pallas as pl
from jax.experimental.pallas import tpu as pltpu
from jax.sharding import PartitionSpec as P

HEADS = 16
HD = 128
STEPS = 50
LATC = 64
NORM_EPS = 1e-06
SHIFT_FACTOR = 7.0
GUIDE_STEP = 0.5

F32 = jnp.float32
BF16 = jnp.bfloat16
VMEM = pl.BlockSpec(memory_space=pltpu.VMEM)
SMEM = pl.BlockSpec(memory_space=pltpu.SMEM)
ANY = pl.BlockSpec(memory_space=pl.ANY)
HBM = pl.BlockSpec(memory_space=pltpu.HBM)
SCORE_SCALE = HD**-0.5 * math.log2(math.e)
NT = (((1,), (1,)), ((), ()))
TN = (((0,), (0,)), ((), ()))


def sigma_at(position):
    frac_left = 1.0 - position / STEPS
    return SHIFT_FACTOR * frac_left / (1.0 + (SHIFT_FACTOR - 1.0) * frac_left)


def normalize(stream):
    average = jnp.mean(stream, axis=-1, keepdims=True)
    centered = stream - average
    inverse = lax.rsqrt(jnp.mean(centered * centered, axis=-1, keepdims=True) + NORM_EPS)
    return centered * inverse, inverse


def pack_kernel(packed, hidden, modulation, sent, passed, rows_of_mod, sems, late):
    heads, kinds, rows, unused = sent.shape
    half = hidden.shape[1] // 2
    copies = []
    for kind in range(kinds):
        for head in range(heads):
            column = (kind * heads + head) * HD
            copies.append(
                pltpu.make_async_copy(
                    packed.at[0, :, pl.ds(column, HD)],
                    sent.at[head, kind],
                    sems.at[kind * heads + head],
                )
            )
    for copy in copies:
        copy.start()
    far = pl.multiple_of((1 - lax.axis_index("cfg") % 2) * half, half)
    rest = pltpu.make_async_copy(
        hidden.at[0, pl.ds(far, half)], passed.at[pl.ds(0, half)], late.at[0]
    )
    rest.start()
    fetch = pltpu.make_async_copy(modulation, rows_of_mod, late.at[1])
    fetch.start()
    fetch.wait()
    mod = jnp.concatenate([rows_of_mod[0], rows_of_mod[1], rows_of_mod[2]], axis=0)
    high = mod.astype(BF16).astype(F32)
    zeros = jnp.zeros((5, mod.shape[1]), F32)
    parts = jnp.concatenate([high, zeros, mod - high, zeros], axis=0)
    passed[pl.ds(half, 16)] = parts.astype(BF16)
    for copy in copies:
        copy.wait()
    rest.wait()


def pack(packed, hidden, modulation):
    rows = packed.shape[1]
    width = hidden.shape[2]
    packed, hidden, modulation = (
        pltpu.with_memory_space_constraint(array, pltpu.HBM)
        for array in (packed, hidden, modulation)
    )
    return pl.pallas_call(
        pack_kernel,
        out_shape=(
            pltpu.VMEM((HEADS, 3, rows, HD), BF16),
            pltpu.VMEM((rows // 2 + 16, width), BF16),
        ),
        in_specs=[HBM, HBM, HBM],
        out_specs=(VMEM, VMEM),
        scratch_shapes=[
            pltpu.VMEM(modulation.shape, F32),
            pltpu.SemaphoreType.DMA((3 * HEADS,)),
            pltpu.SemaphoreType.DMA((2,)),
        ],
        compiler_params=pltpu.CompilerParams(vmem_limit_bytes=16 << 20),
    )(packed, hidden, modulation)


QBLOCK = 512


def split_query(own, first, count):
    query = own[pl.ds(first, count), 0].reshape(QBLOCK, HD).astype(F32) * SCORE_SCALE
    high = query.astype(BF16)
    low = (query - high.astype(F32)).astype(BF16)
    return jnp.concatenate([high, low], axis=1)


def place_pair(keys, values, first, key, value):
    span = pl.ds(first, key.shape[0])
    keys[span, :HD] = key
    keys[span, HD:] = key
    values[:HD, span] = value.T


def run_steps(steps, score, finish):
    score(0, 0)
    for step in range(steps):
        if step + 1 < steps:
            score(step + 1, (step + 1) % 2)
        finish(step, step % 2)


def near_kernel(own, state, keys, values, scores, tops):
    sources, unused, rows, unused2 = own.shape
    video = sources * rows
    place_pair(keys, values, 0, own[:, 1].reshape(video, HD), own[:, 2].reshape(video, HD))
    values[HD:, :] = jnp.ones((values.shape[0] - HD, video), BF16)
    count = QBLOCK // rows

    def score(step, slot):
        got = lax.dot_general(
            keys[...], split_query(own, step * count, count), NT, preferred_element_type=F32
        )
        scores[slot] = got
        tops[slot] = jnp.max(got, axis=0, keepdims=True)

    def finish(step, slot):
        highest = tops[slot]
        weights = jnp.exp2(scores[slot] - highest).astype(BF16)
        mixed = jnp.dot(values[...], weights, preferred_element_type=F32)
        span = pl.ds(step * QBLOCK, QBLOCK)
        state[: HD + 8, span] = mixed[: HD + 8]
        state[HD + 8 :, span] = jnp.broadcast_to(highest, (8, QBLOCK))

    run_steps(video // QBLOCK, score, finish)


def far_kernel(
    own, other, state, text_kv, length, weight, out, staged, keys, values, scores, tops, text, sems
):
    head = lax.axis_index("seq") // (lax.axis_size("seq") // HEADS)
    text_copies = [
        pltpu.make_async_copy(
            text_kv.at[0, :, pl.ds(pl.multiple_of((kind * HEADS + head) * HD, HD), HD)],
            text.at[kind],
            sems.at[1 + kind],
        )
        for kind in range(2)
    ]
    for copy in text_copies:
        copy.start()
    staging = pltpu.make_async_copy(weight, staged, sems.at[0])
    staging.start()
    sources, unused, rows, unused2 = own.shape
    video = sources * rows
    words = text.shape[1]
    place_pair(keys, values, 0, other[:, 1].reshape(video, HD), other[:, 2].reshape(video, HD))
    for copy in text_copies:
        copy.wait()
    place_pair(keys, values, video, text[0], text[1])
    values[HD:, :] = jnp.ones((values.shape[0] - HD, video + words), BF16)
    kept = lax.broadcasted_iota(jnp.int32, (words, QBLOCK), 0) < length[0]
    count = QBLOCK // rows

    def score(step, slot):
        got = lax.dot_general(
            keys[...], split_query(own, step * count, count), NT, preferred_element_type=F32
        )
        masked = jnp.where(kept, got[video:], -jnp.inf)
        scores[slot, :video] = got[:video]
        scores[slot, video:] = masked
        tops[slot] = jnp.maximum(
            jnp.max(got[:video], axis=0, keepdims=True), jnp.max(masked, axis=0, keepdims=True)
        )

    def finish(step, slot):
        span = pl.ds(step * QBLOCK, QBLOCK)
        before = state[HD + 8 : HD + 9, span]
        highest = jnp.maximum(tops[slot], before)
        weights = jnp.exp2(scores[slot] - highest).astype(BF16)
        mixed = jnp.dot(values[...], weights, preferred_element_type=F32)
        mixed = mixed[: HD + 8] + state[: HD + 8, span] * jnp.exp2(before - highest)
        result = (mixed[:HD] / mixed[HD : HD + 1]).T.astype(BF16)
        result = result.reshape(count, 2, rows // 2, HD)
        span = pl.ds(step * count, count)
        out[0, span] = result[:, 0]
        out[1, span] = result[:, 1]

    run_steps(video // QBLOCK, score, finish)
    staging.wait()


def attend_near(own):
    sources, unused, rows, unused2 = own.shape
    total = sources * rows
    return pl.pallas_call(
        near_kernel,
        out_shape=jax.ShapeDtypeStruct((HD + 16, total), F32),
        in_specs=[VMEM],
        out_specs=VMEM,
        scratch_shapes=[
            pltpu.VMEM((total, 2 * HD), BF16),
            pltpu.VMEM((HD + 16, total), BF16),
            pltpu.VMEM((2, total, QBLOCK), F32),
            pltpu.VMEM((2, 1, QBLOCK), F32),
        ],
        compiler_params=pltpu.CompilerParams(vmem_limit_bytes=28 << 20),
        cost_estimate=pl.CostEstimate(flops=5 << 30, bytes_accessed=4 << 20, transcendentals=0),
    )(own)


def attend_far(own, other, state, text_kv, length, weight):
    sources, unused, rows, unused2 = own.shape
    words = text_kv.shape[1]
    total = sources * rows + words
    return pl.pallas_call(
        far_kernel,
        out_shape=(
            jax.ShapeDtypeStruct((2, sources, rows // 2, HD), BF16),
            pltpu.VMEM(weight.shape, BF16),
        ),
        in_specs=[VMEM, VMEM, VMEM, ANY, SMEM, ANY],
        out_specs=(VMEM, VMEM),
        scratch_shapes=[
            pltpu.VMEM((total, 2 * HD), BF16),
            pltpu.VMEM((HD + 16, total), BF16),
            pltpu.VMEM((2, total, QBLOCK), F32),
            pltpu.VMEM((2, 1, QBLOCK), F32),
            pltpu.VMEM((2, words, HD), BF16),
            pltpu.SemaphoreType.DMA((3,)),
        ],
        compiler_params=pltpu.CompilerParams(vmem_limit_bytes=40 << 20),
        cost_estimate=pl.CostEstimate(flops=5 << 30, bytes_accessed=12 << 20, transcendentals=0),
    )(own, other, state, text_kv, length, weight)


def final_kernel(
    levels, times, heads, weight, hidden, got, modulation, guide_table, final_t, latent,
    next_out, guided_out, kept_out, sent_out, attention,
    *, count_scale,
):
    width = weight.shape[1]
    cfg_index = lax.axis_index("cfg")
    core = lax.axis_index("seq") % (lax.axis_size("seq") // HEADS)
    branch = cfg_index % 2
    is_cond = branch == 0
    level = levels[cfg_index // 2]
    half = hidden.shape[1] // 2
    for side in range(2):
        for head in range(HEADS):
            attention[pl.ds(side * half, half), pl.ds(head * HD, HD)] = heads[
                side * HEADS + head
            ]
    projected = jnp.dot(attention[...], weight[...], preferred_element_type=F32)
    projected = projected.astype(BF16).astype(F32)
    own_h = hidden[0, pl.ds(pl.multiple_of(branch * half, half), half)].astype(F32)
    got_h = got[:half].astype(F32)
    own_mod = jnp.concatenate([modulation[0], modulation[1], modulation[2]], axis=0)
    parts = got[half:].astype(F32)
    got_mod = parts[:3] + parts[8:11]
    cond_hidden = jnp.where(is_cond, own_h, got_h)
    uncond_hidden = jnp.where(is_cond, got_h, own_h)
    cond_mod = jnp.where(is_cond, own_mod, got_mod)
    uncond_mod = jnp.where(is_cond, got_mod, own_mod)
    cond_proj = projected[:half]

    def layer(hidden, proj, mod):
        normed, inverse = normalize(hidden + mod[0:1] * proj)
        shaped = (normed * (1.0 + mod[2:3]) + mod[1:2]).astype(BF16)
        velocity = lax.dot_general(shaped, final_t[...], NT, preferred_element_type=F32)
        return normed, inverse, shaped, velocity

    cond_vel = layer(cond_hidden, cond_proj, cond_mod)[3]
    uncond_vel = layer(uncond_hidden, projected[half:], uncond_mod)[3]
    factor = 1.0 + GUIDE_STEP * level.astype(F32)
    guided = uncond_vel + factor * (cond_vel - uncond_vel)
    guided_out[0] = guided
    position = jnp.full(guided.shape, times[cfg_index // 2].astype(F32))
    next_out[0] = latent[0] + (sigma_at(position + 1.0) - sigma_at(position)) * guided

    mod = cond_mod + guide_table[level]
    normed, inverse, shaped, velocity = layer(cond_hidden, cond_proj, mod)
    grad_vel = ((velocity - guided) * count_scale).astype(BF16)
    grad_shaped = jnp.dot(grad_vel, final_t[...], preferred_element_type=F32)
    grad_shift = jnp.sum(grad_shaped, axis=0, keepdims=True)
    grad_scale = jnp.sum(grad_shaped * normed, axis=0, keepdims=True)
    grad_norm = grad_shaped * (1.0 + mod[2:3])
    grad_stream = inverse * (
        grad_norm
        - jnp.mean(grad_norm, axis=1, keepdims=True)
        - normed * jnp.mean(grad_norm * normed, axis=1, keepdims=True)
    )
    grad_gate = jnp.sum(grad_stream * cond_proj, axis=0, keepdims=True)
    table = jnp.concatenate(
        [grad_gate, grad_shift, grad_scale, jnp.zeros((13, width), F32)], axis=0
    ).astype(BF16)
    left = jnp.concatenate([shaped, table], axis=0)
    lanes = lax.broadcasted_iota(jnp.int32, (16, 2 * LATC), 1)
    lines = lax.broadcasted_iota(jnp.int32, (16, 2 * LATC), 0)
    unit = (lanes == lines + LATC).astype(F32).astype(BF16)
    right = jnp.concatenate(
        [jnp.concatenate([grad_vel, jnp.zeros_like(grad_vel)], axis=1), unit], axis=0
    )
    terms = lax.dot_general(left, right, TN, preferred_element_type=F32)
    terms = terms.reshape(width // 16, 2, 8, 2 * LATC)
    first = terms[:, 0].reshape(width // 2, 2 * LATC)
    second = terms[:, 1].reshape(width // 2, 2 * LATC)
    on_first = core == 0
    kept_out[...] = jnp.where(on_first, first, second)
    sent_out[...] = jnp.where(on_first, second, first).astype(BF16)


def final_layer(
    levels, times, heads, weight, hidden, got, modulation, guide_table, final_t, latent, count_scale
):
    width = hidden.shape[2]
    half = hidden.shape[1] // 2
    return pl.pallas_call(
        functools.partial(final_kernel, count_scale=count_scale),
        out_shape=(
            jax.ShapeDtypeStruct(latent.shape, F32),
            jax.ShapeDtypeStruct(latent.shape, F32),
            jax.ShapeDtypeStruct((width // 2, 2 * LATC), F32),
            jax.ShapeDtypeStruct((width // 2, 2 * LATC), BF16),
        ),
        in_specs=[SMEM, SMEM] + [VMEM] * 8,
        out_specs=(VMEM, VMEM, VMEM, VMEM),
        scratch_shapes=[pltpu.VMEM((2 * half, HEADS * HD), BF16)],
        compiler_params=pltpu.CompilerParams(vmem_limit_bytes=32 << 20),
        cost_estimate=pl.CostEstimate(flops=1 << 30, bytes_accessed=10 << 20, transcendentals=0),
    )(levels, times, heads, weight, hidden, got, modulation, guide_table, final_t, latent)


def sum_kernel(levels, got, final_out, table_out):
    clips = got.shape[0]
    guides = table_out.shape[2]
    total = None
    planes = [jnp.zeros((8, guides), F32) for unused in range(3)]
    for clip in range(clips):
        block = got[clip].astype(F32).reshape(got.shape[1] // 8, 8, 2 * LATC)
        block = jnp.sum(block, axis=0)
        total = block if total is None else total + block
        picked = lax.broadcasted_iota(jnp.int32, (8, guides), 1) == levels[clip]
        for plane in range(3):
            column = block[:, LATC + plane : LATC + plane + 1]
            planes[plane] = planes[plane] + jnp.where(picked, column, 0.0)
    final_out[...] = total[:, :LATC]
    for plane in range(3):
        table_out[plane] = planes[plane]


def sum_terms(levels, got, guides):
    return pl.pallas_call(
        sum_kernel,
        out_shape=(
            jax.ShapeDtypeStruct((8, LATC), F32),
            jax.ShapeDtypeStruct((3, 8, guides), F32),
        ),
        in_specs=[SMEM, VMEM],
        out_specs=(VMEM, VMEM),
        compiler_params=pltpu.CompilerParams(vmem_limit_bytes=16 << 20),
    )(levels, got)


def local(
    latent,
    query_key_value,
    text_kv,
    text_len,
    hidden,
    modulation,
    out_weight,
    final_weight,
    guide_table,
    time_index,
    guide_index,
):
    seq_count = lax.axis_size("seq")
    cfg_count = lax.axis_size("cfg")
    clips = cfg_count // 2
    tok_rows = query_key_value.shape[1]
    half_rows = tok_rows // 2
    cores = seq_count // HEADS
    mod_rows = modulation.transpose(1, 0, 2)

    sent, passed = pack(query_key_value, hidden, mod_rows)
    same_core = [[cores * i + core for i in range(HEADS)] for core in range(cores)]
    got = lax.all_to_all(
        sent.reshape(HEADS, 3 * tok_rows, HD),
        "seq",
        split_axis=0,
        concat_axis=0,
        tiled=True,
        axis_index_groups=same_core,
    )
    own = got.reshape(HEADS, 3, tok_rows, HD)
    other = lax.ppermute(own, "seq", [(i, i ^ 1) for i in range(seq_count)])
    gotten = lax.ppermute(passed, "cfg", [(i, i ^ 1) for i in range(cfg_count)])
    state = attend_near(own)
    mixed, weight = attend_far(own, other, state, text_kv, text_len, out_weight)
    mixed, gotten = lax.optimization_barrier((mixed, gotten))

    members = 2 * HEADS
    groups = [
        [(g * members + i) * cores + core for i in range(members)]
        for g in range(clips)
        for core in range(cores)
    ]
    heads = lax.all_to_all(
        mixed.reshape(members, half_rows, HD),
        ("cfg", "seq"),
        split_axis=0,
        concat_axis=0,
        tiled=True,
        axis_index_groups=groups,
    )

    count_scale = 1.0 / (clips * tok_rows * seq_count)
    latent_next, guided, kept, given = final_layer(
        guide_index,
        time_index,
        heads,
        weight,
        hidden,
        gotten,
        mod_rows,
        guide_table,
        final_weight.T,
        latent,
        count_scale,
    )
    gained = lax.ppermute(given, "seq", [(i, i ^ 1) for i in range(seq_count)])
    chips = cfg_count * seq_count // cores
    terms = (kept + gained.astype(F32)).astype(BF16)
    pieces = lax.all_to_all(
        terms.reshape(chips, terms.shape[0] // chips, 2 * LATC),
        ("cfg", "seq"),
        split_axis=0,
        concat_axis=0,
        tiled=True,
        axis_index_groups=[[cores * i + core for i in range(chips)] for core in range(cores)],
    )
    final_grad, table = sum_terms(
        guide_index, pieces.reshape(clips, terms.shape[0] // clips, 2 * LATC), guide_table.shape[0]
    )
    return (latent_next, guided, final_grad, table.transpose(2, 0, 1))


def solution(mesh):
    in_specs = (
        P("cfg", "seq", None),
        P("cfg", "seq", None),
        P("cfg", None, None),
        P("cfg"),
        P("cfg", "seq", None),
        P("cfg", None, None),
        P(),
        P(),
        P(),
        P(),
        P(),
    )
    out_specs = (
        P("cfg", "seq", None),
        P("cfg", "seq", None),
        P(("cfg", "seq"), None),
        P(None, None, ("cfg", "seq")),
    )
    return jax.shard_map(local, mesh=mesh, in_specs=in_specs, out_specs=out_specs, check_vma=False)
```

profile of v0, /device:TPU:2, one launch (start us, length us, event | category | flops | bytes accessed | tf_op | source)
XLA Modules:
  0.0 118.5 jit_solution(5356363259420270365)
XLA Ops:
  0.6 2.0 %shard_map.138 = (bf16[16,3,128,128]{3,2,1,0:T(8,128)(2,1)S(1)}, bf16[80,2048]{1,0:T(8,128)(2,1)S(1)}) custom-call(bf16[1,128,6144]{2,1,0:T(8,128)(2,1)} %packed.1, bf16[1,128,2048]{2,1,0:T(8,128)(2,1)} %hidden.3, f32[3,1,2048]{2,1,0:T(1,128)} %bitcast.16), custom_call_target="tpu_custom_call" | custom-call | tf_op jit(solution)/shard_map/pallas_call | solution.py:83
  2.7 52.1 %all_to_all.15 = bf16[16,384,128]{2,1,0:T(8,128)(2,1)S(1)} all-to-all(bf16[16,384,128]{2,1,0:T(8,128)(2,1)S(1)} %bitcast.12), channel_id=1, replica_groups={{0,2,4,6,8,10,12,14,16,18,20,22,24,26,28,30},{1,3,5,7,9,11,13,15,17,19,..., dimensions={0} | all-to-all | bytes 3145728 | tf_op jit(solution)/shard_map/all_to_all | solution.py:400
  54.8 0.0 collective-permute-start
  54.8 0.7 collective-permute-start.1
  56.2 0.0 copy-start.7
  56.2 5.1 %shard_map.139.state = f32[144,2048]{1,0:T(8,128)S(1)} custom-call(bf16[16,3,128,128]{3,2,1,0:T(8,128)(2,1)S(1)} %bitcast.10), custom_call_target="tpu_custom_call" | custom-call | flops 5368709120 | bytes 4194304 | tf_op jit(solution)/shard_map/pallas_call | solution.py:208
  61.3 0.0 copy-start
  61.3 0.0 copy-start.1
  61.3 0.0 copy-start.2
  61.3 0.0 copy-start.3
  61.3 0.0 copy-start.4
  61.4 0.0 copy-start.5
  61.4 0.0 copy-start.6
  61.4 0.0 collective-permute-done.other
  61.4 6.0 %shard_map.140 = (bf16[2,16,64,128]{3,2,1,0:T(8,128)(2,1)S(1)}, bf16[2048,2048]{1,0:T(8,128)(2,1)S(1)}) custom-call(bf16[16,3,128,128]{3,2,1,0:T(8,128)(2,1)S(1)} %bitcast.11, bf16[16,3,128,128]{3,2,1,0:T(8,128)(2,1)S(1)} %collective-permute-done.other, f32[144,2048]{1,0:T(8,128)S(1)} %shard_map.139.state, bf16[1,128,4096]{2,1,0:T(8,128)(2,1)S(1)} %copy-done.7, ...), custom_call_target="tpu_custom_call" | custom-call | flops 5368709120 | bytes 12582912 | tf_op jit(solution)/shard_map/pallas_call | solution.py:228
  67.4 0.0 collective-permute-done.1.got
  67.4 21.9 %all_to_all.16.heads = bf16[32,64,128]{2,1,0:T(8,128)(2,1)S(1)} all-to-all(bf16[32,64,128]{2,1,0:T(8,128)(2,1)S(1)} %bitcast.14), channel_id=1, replica_groups={{0,2,4,6,8,10,12,14,16,18,20,22,24,26,28,30,32,34,36,38,40,42,44,46,48,..., dimensions={0} | all-to-all | bytes 1048576 | tf_op jit(solution)/shard_map/all_to_all | solution.py:421
  89.3 0.0 copy-done
  89.4 3.3 %shard_map.141 = (f32[1,64,64]{2,1,0:T(8,128)}, f32[1,64,64]{2,1,0:T(8,128)}, f32[1024,128]{1,0:T(8,128)S(1)}, bf16[1024,128]{1,0:T(8,128)(2,1)S(1)}) custom-call(s32[4]{0:T(128)S(1)} %copy-done.5, s32[4]{0:T(128)S(1)} %copy-done.6, bf16[32,64,128]{2,1,0:T(8,128)(2,1)S(1)} %all_to_all.16.heads, bf16[2048,2048]{1,0:T(8,128)(2,1)S(1)} %get-tuple-element.20.weight, ...), custom_call_target="tpu_custom_call" | custom-call | flops 1073741824 | bytes 10485760 | tf_op jit(solution)/shard_map/pallas_call | solution.py:330
  92.7 0.1 collective-permute-start.2
  92.8 1.5 %collective-permute-done.2 = bf16[1024,128]{1,0:T(8,128)(2,1)S(1)} collective-permute-done((bf16[1024,128]{1,0:T(8,128)(2,1)S(1)}, bf16[1024,128]{1,0:T(8,128)(2,1)S(1)}, u32[]{:S(2)}, u32[]{:S(2)}) %collective-permute-start.2) | collective-permute-done | bytes 262176 | tf_op jit(solution)/shard_map/ppermute | solution.py:444
  94.3 0.1 fusion
  94.3 22.9 %all_to_all.17 = bf16[128,8,128]{2,1,0:T(8,128)(2,1)S(1)} all-to-all(bf16[128,8,128]{2,1,0:T(8,128)(2,1)S(1)} %fusion), channel_id=1, replica_groups={{0,2,4,6,8,10,12,14,16,18,20,22,24,26,28,30,32,34,36,38,40,42,44,46,48,..., dimensions={0} | all-to-all | bytes 524288 | tf_op jit(solution)/shard_map/all_to_all | solution.py:447
  117.2 1.3 %shard_map.142 = (f32[8,64]{1,0:T(8,128)}, f32[3,8,12]{2,1,0:T(8,128)}) custom-call(s32[4]{0:T(128)S(1)} %copy-done.5, bf16[4,256,128]{2,1,0:T(8,128)(2,1)S(1)} %bitcast.13), custom_call_target="tpu_custom_call" | custom-call | tf_op jit(solution)/shard_map/pallas_call | solution.py:365
  (7 shorter events, 0.0 us)
Async XLA Ops:
  54.8 6.6 %collective-permute-start = (bf16[16,3,128,128]{3,2,1,0:T(8,128)(2,1)S(1)}, bf16[16,3,128,128]{3,2,1,0:T(8,128)(2,1)S(1)}, u32[]{:S(2)}, u32[]{:S(2)}) collective-permute-start(bf16[16,3,128,128]{3,2,1,0:T(8,128)(2,1)S(1)} %bitcast.9), channel_id=1, source_target_pairs={{0,1},{1,0},{2,3},{3,2},{4,5},{5,4},{6,7},{7,6},{8,9},{9,8},{10,11... | collective-permute-start | bytes 4718600 | tf_op jit(solution)/shard_map/ppermute | solution.py:409
  54.8 12.6 %collective-permute-start.1 = (bf16[80,2048]{1,0:T(8,128)(2,1)S(1)}, bf16[80,2048]{1,0:T(8,128)(2,1)S(1)}, u32[]{:S(2)}, u32[]{:S(2)}) collective-permute-start(bf16[80,2048]{1,0:T(8,128)(2,1)S(1)} %get-tuple-element.18), channel_id=1, source_target_pairs={{0,32},{32,0},{64,96},{96,64},{128,160},{160,128},{192,224},{224,1... | collective-permute-start | bytes 983048 | tf_op jit(solution)/shard_map/ppermute | solution.py:410
  56.2 5.2 %copy-start.7 = (bf16[1,128,4096]{2,1,0:T(8,128)(2,1)S(1)}, bf16[1,128,4096]{2,1,0:T(8,128)(2,1)}, u32[]{:S(2)}) copy-start(bf16[1,128,4096]{2,1,0:T(8,128)(2,1)} %text_kv.1) | copy-start | bytes 3145732
  61.3 28.0 %copy-start = (bf16[1,128,2048]{2,1,0:T(8,128)(2,1)S(1)}, bf16[1,128,2048]{2,1,0:T(8,128)(2,1)}, u32[]{:S(2)}) copy-start(bf16[1,128,2048]{2,1,0:T(8,128)(2,1)} %hidden.3) | copy-start | bytes 1572868
  61.3 28.0 %copy-start.1 = (f32[12,3,2048]{2,1,0:T(4,128)S(1)}, f32[12,3,2048]{2,1,0:T(4,128)}, u32[]{:S(2)}) copy-start(f32[12,3,2048]{2,1,0:T(4,128)} %guide_table.1) | copy-start | bytes 884740
  61.3 28.0 %copy-start.2 = (bf16[2048,64]{0,1:T(8,128)(2,1)S(1)}, bf16[2048,64]{0,1:T(8,128)(2,1)}, u32[]{:S(2)}) copy-start(bf16[2048,64]{0,1:T(8,128)(2,1)} %param.18) | copy-start | bytes 786436
  61.3 28.0 %copy-start.3 = (f32[1,3,2048]{2,0,1:T(1,128)S(1)}, f32[1,3,2048]{2,0,1:T(1,128)}, u32[]{:S(2)}) copy-start(f32[1,3,2048]{2,0,1:T(1,128)} %param.16) | copy-start | bytes 73732
  61.3 28.0 %copy-start.4 = (f32[1,64,64]{2,1,0:T(8,128)S(1)}, f32[1,64,64]{2,1,0:T(8,128)}, u32[]{:S(2)}) copy-start(f32[1,64,64]{2,1,0:T(8,128)} %latent.1) | copy-start | bytes 49156
  61.4 28.0 %copy-start.5 = (s32[4]{0:T(128)S(1)}, s32[4]{0:T(128)}, u32[]{:S(2)}) copy-start(s32[4]{0:T(128)} %levels.3) | copy-start | bytes 52
  61.4 28.0 %copy-start.6 = (s32[4]{0:T(128)S(1)}, s32[4]{0:T(128)}, u32[]{:S(2)}) copy-start(s32[4]{0:T(128)} %times.1) | copy-start | bytes 52
  92.7 1.6 %collective-permute-start.2 = (bf16[1024,128]{1,0:T(8,128)(2,1)S(1)}, bf16[1024,128]{1,0:T(8,128)(2,1)S(1)}, u32[]{:S(2)}, u32[]{:S(2)}) collective-permute-start(bf16[1024,128]{1,0:T(8,128)(2,1)S(1)} %get-tuple-element.25), channel_id=1, source_target_pairs={{0,1},{1,0},{2,3},{3,2},{4,5},{5,4},{6,7},{7,6},{8,9},{9,8},{10,11... | collective-permute-start | bytes 786440 | tf_op jit(solution)/shard_map/ppermute | solution.py:444
where the time goes:
time: 119 us; the launch traced here: 118 us
  blocking collectives  96.9 us (81%)
  Pallas kernels  17.7 us (15%)
  waiting for transfers between devices  1.53 us (1%)
  between operations  1.45 us (1%)
    all_to_all x1, blocking collectives, local(): lax.all_to_all(sent.reshape(HEADS, 3 * tok_rows, HD), 'seq', split_axis=0...  52.1 us
    all_to_all x1, blocking collectives, local(): lax.all_to_all(terms.reshape(chips, terms.shape[0] // chips, 2 * LATC), (...  22.9 us
    all_to_all x1, blocking collectives, local(): lax.all_to_all(mixed.reshape(members, half_rows, HD), ('cfg', 'seq'), spl...  21.9 us
    pallas_call x1, Pallas kernels, attend_far(): pl.pallas_call(far_kernel, out_shape=(jax.ShapeDtypeStruct((2, sources, r...  5.99 us
    pallas_call x1, Pallas kernels, attend_near(): pl.pallas_call(near_kernel, out_shape=jax.ShapeDtypeStruct((HD + 16, tota...  5.12 us
    pallas_call x1, Pallas kernels, final_layer(): pl.pallas_call(functools.partial(final_kernel, count_scale=count_scale),...  3.28 us
  transfers between devices with their start and end apart: 3, of which 1 were waited for; matrix products, arithmetic and copies ran while one was open for 0% of the time, Pallas kernels for 9%

commit v1 on v0

--- a/solution.py
+++ b/solution.py
@@ -39,20 +39,21 @@
     return centered * inverse, inverse
 
 
-def pack_kernel(packed, hidden, modulation, sent, passed, rows_of_mod, sems, late):
+PIECES = 8
+
+
+def pack_kernel(packed, hidden, modulation, sent, passed, rows_of_mod, held, sems, late):
     heads, kinds, rows, unused = sent.shape
     half = hidden.shape[1] // 2
-    copies = []
-    for kind in range(kinds):
-        for head in range(heads):
-            column = (kind * heads + head) * HD
-            copies.append(
-                pltpu.make_async_copy(
-                    packed.at[0, :, pl.ds(column, HD)],
-                    sent.at[head, kind],
-                    sems.at[kind * heads + head],
-                )
-            )
+    piece = rows // PIECES
+    copies = [
+        pltpu.make_async_copy(
+            packed.at[0, pl.ds(index * piece, piece)],
+            held.at[pl.ds(index * piece, piece)],
+            sems.at[index],
+        )
+        for index in range(PIECES)
+    ]
     for copy in copies:
         copy.start()
     far = pl.multiple_of((1 - lax.axis_index("cfg") % 2) * half, half)
@@ -68,8 +69,13 @@
     zeros = jnp.zeros((5, mod.shape[1]), F32)
     parts = jnp.concatenate([high, zeros, mod - high, zeros], axis=0)
     passed[pl.ds(half, 16)] = parts.astype(BF16)
-    for copy in copies:
-        copy.wait()
+    for index in range(PIECES):
+        copies[index].wait()
+        span = pl.ds(index * piece, piece)
+        for kind in range(kinds):
+            for head in range(heads):
+                column = (kind * heads + head) * HD
+                sent[head, kind, span] = held[span, pl.ds(column, HD)]
     rest.wait()
 
 
@@ -90,7 +96,8 @@
         out_specs=(VMEM, VMEM),
         scratch_shapes=[
             pltpu.VMEM(modulation.shape, F32),
-            pltpu.SemaphoreType.DMA((3 * HEADS,)),
+            pltpu.VMEM(packed.shape[1:], BF16),
+            pltpu.SemaphoreType.DMA((PIECES,)),
             pltpu.SemaphoreType.DMA((2,)),
         ],
         compiler_params=pltpu.CompilerParams(vmem_limit_bytes=16 << 20),

time: 119 us -> 118 us (level)
  no operation moved by 1% of the time
where the time goes in v1:
time: 118 us
  blocking collectives  96.9 us (82%)
  Pallas kernels  17.4 us (15%)
  waiting for transfers between devices  1.53 us (1%)
  between operations  1.45 us (1%)
    all_to_all x1, blocking collectives, local(): lax.all_to_all(sent.reshape(HEADS, 3 * tok_rows, HD), 'seq', split_axis=0...  52.1 us
    all_to_all x1, blocking collectives, local(): lax.all_to_all(terms.reshape(chips, terms.shape[0] // chips, 2 * LATC), (...  22.9 us
    all_to_all x1, blocking collectives, local(): lax.all_to_all(mixed.reshape(members, half_rows, HD), ('cfg', 'seq'), spl...  21.9 us
    pallas_call x1, Pallas kernels, attend_far(): pl.pallas_call(far_kernel, out_shape=(jax.ShapeDtypeStruct((2, sources, r...  5.99 us
    pallas_call x1, Pallas kernels, attend_near(): pl.pallas_call(near_kernel, out_shape=jax.ShapeDtypeStruct((HD + 16, tota...  5.12 us
    pallas_call x1, Pallas kernels, final_layer(): pl.pallas_call(functools.partial(final_kernel, count_scale=count_scale),...  3.28 us
  transfers between devices with their start and end apart: 3, of which 1 were waited for; matrix products, arithmetic and copies ran while one was open for 0% of the time, Pallas kernels for 9%

profile of v1, /device:TPU:2, one launch (start us, length us, event | category | flops | bytes accessed | tf_op | source)
XLA Modules:
  0.0 118.2 jit_solution(415817874688392552)
XLA Ops:
  0.6 1.8 %shard_map.138 = (bf16[16,3,128,128]{3,2,1,0:T(8,128)(2,1)S(1)}, bf16[80,2048]{1,0:T(8,128)(2,1)S(1)}) custom-call(bf16[1,128,6144]{2,1,0:T(8,128)(2,1)} %packed.1, bf16[1,128,2048]{2,1,0:T(8,128)(2,1)} %hidden.3, f32[3,1,2048]{2,1,0:T(1,128)} %bitcast.16), custom_call_target="tpu_custom_call" | custom-call | tf_op jit(solution)/shard_map/pallas_call | solution.py:89
  2.4 52.1 %all_to_all.15 = bf16[16,384,128]{2,1,0:T(8,128)(2,1)S(1)} all-to-all(bf16[16,384,128]{2,1,0:T(8,128)(2,1)S(1)} %bitcast.12), channel_id=1, replica_groups={{0,2,4,6,8,10,12,14,16,18,20,22,24,26,28,30},{1,3,5,7,9,11,13,15,17,19,..., dimensions={0} | all-to-all | bytes 3145728 | tf_op jit(solution)/shard_map/all_to_all | solution.py:407
  54.6 0.0 collective-permute-start
  54.6 0.7 collective-permute-start.1
  55.9 0.0 copy-start.7
  55.9 5.1 %shard_map.139.state = f32[144,2048]{1,0:T(8,128)S(1)} custom-call(bf16[16,3,128,128]{3,2,1,0:T(8,128)(2,1)S(1)} %bitcast.10), custom_call_target="tpu_custom_call" | custom-call | flops 5368709120 | bytes 4194304 | tf_op jit(solution)/shard_map/pallas_call | solution.py:215
  61.0 0.0 copy-start
  61.0 0.0 copy-start.1
  61.1 0.0 copy-start.2
  61.1 0.0 copy-start.3
  61.1 0.0 copy-start.4
  61.1 0.0 copy-start.5
  61.1 0.0 copy-start.6
  61.1 0.0 collective-permute-done.other
  61.1 6.0 %shard_map.140 = (bf16[2,16,64,128]{3,2,1,0:T(8,128)(2,1)S(1)}, bf16[2048,2048]{1,0:T(8,128)(2,1)S(1)}) custom-call(bf16[16,3,128,128]{3,2,1,0:T(8,128)(2,1)S(1)} %bitcast.11, bf16[16,3,128,128]{3,2,1,0:T(8,128)(2,1)S(1)} %collective-permute-done.other, f32[144,2048]{1,0:T(8,128)S(1)} %shard_map.139.state, bf16[1,128,4096]{2,1,0:T(8,128)(2,1)S(1)} %copy-done.7, ...), custom_call_target="tpu_custom_call" | custom-call | flops 5368709120 | bytes 12582912 | tf_op jit(solution)/shard_map/pallas_call | solution.py:235
  67.1 0.0 collective-permute-done.1.got
  67.1 21.9 %all_to_all.16.heads = bf16[32,64,128]{2,1,0:T(8,128)(2,1)S(1)} all-to-all(bf16[32,64,128]{2,1,0:T(8,128)(2,1)S(1)} %bitcast.14), channel_id=1, replica_groups={{0,2,4,6,8,10,12,14,16,18,20,22,24,26,28,30,32,34,36,38,40,42,44,46,48,..., dimensions={0} | all-to-all | bytes 1048576 | tf_op jit(solution)/shard_map/all_to_all | solution.py:428
  89.1 0.0 copy-done.3
  89.1 3.3 %shard_map.141 = (f32[1,64,64]{2,1,0:T(8,128)}, f32[1,64,64]{2,1,0:T(8,128)}, f32[1024,128]{1,0:T(8,128)S(1)}, bf16[1024,128]{1,0:T(8,128)(2,1)S(1)}) custom-call(s32[4]{0:T(128)S(1)} %copy-done.5, s32[4]{0:T(128)S(1)} %copy-done.6, bf16[32,64,128]{2,1,0:T(8,128)(2,1)S(1)} %all_to_all.16.heads, bf16[2048,2048]{1,0:T(8,128)(2,1)S(1)} %get-tuple-element.20.weight, ...), custom_call_target="tpu_custom_call" | custom-call | flops 1073741824 | bytes 10485760 | tf_op jit(solution)/shard_map/pallas_call | solution.py:337
  92.4 0.1 collective-permute-start.2
  92.5 1.5 %collective-permute-done.2 = bf16[1024,128]{1,0:T(8,128)(2,1)S(1)} collective-permute-done((bf16[1024,128]{1,0:T(8,128)(2,1)S(1)}, bf16[1024,128]{1,0:T(8,128)(2,1)S(1)}, u32[]{:S(2)}, u32[]{:S(2)}) %collective-permute-start.2) | collective-permute-done | bytes 262176 | tf_op jit(solution)/shard_map/ppermute | solution.py:451
  94.0 0.1 fusion
  94.1 22.9 %all_to_all.17 = bf16[128,8,128]{2,1,0:T(8,128)(2,1)S(1)} all-to-all(bf16[128,8,128]{2,1,0:T(8,128)(2,1)S(1)} %fusion), channel_id=1, replica_groups={{0,2,4,6,8,10,12,14,16,18,20,22,24,26,28,30,32,34,36,38,40,42,44,46,48,..., dimensions={0} | all-to-all | bytes 524288 | tf_op jit(solution)/shard_map/all_to_all | solution.py:454
  117.0 1.3 %shard_map.142 = (f32[8,64]{1,0:T(8,128)}, f32[3,8,12]{2,1,0:T(8,128)}) custom-call(s32[4]{0:T(128)S(1)} %copy-done.5, bf16[4,256,128]{2,1,0:T(8,128)(2,1)S(1)} %bitcast.13), custom_call_target="tpu_custom_call" | custom-call | tf_op jit(solution)/shard_map/pallas_call | solution.py:372
  (7 shorter events, 0.0 us)
Async XLA Ops:
  54.6 6.6 %collective-permute-start = (bf16[16,3,128,128]{3,2,1,0:T(8,128)(2,1)S(1)}, bf16[16,3,128,128]{3,2,1,0:T(8,128)(2,1)S(1)}, u32[]{:S(2)}, u32[]{:S(2)}) collective-permute-start(bf16[16,3,128,128]{3,2,1,0:T(8,128)(2,1)S(1)} %bitcast.9), channel_id=1, source_target_pairs={{0,1},{1,0},{2,3},{3,2},{4,5},{5,4},{6,7},{7,6},{8,9},{9,8},{10,11... | collective-permute-start | bytes 4718600 | tf_op jit(solution)/shard_map/ppermute | solution.py:416
  54.6 12.6 %collective-permute-start.1 = (bf16[80,2048]{1,0:T(8,128)(2,1)S(1)}, bf16[80,2048]{1,0:T(8,128)(2,1)S(1)}, u32[]{:S(2)}, u32[]{:S(2)}) collective-permute-start(bf16[80,2048]{1,0:T(8,128)(2,1)S(1)} %get-tuple-element.18), channel_id=1, source_target_pairs={{0,32},{32,0},{64,96},{96,64},{128,160},{160,128},{192,224},{224,1... | collective-permute-start | bytes 983048 | tf_op jit(solution)/shard_map/ppermute | solution.py:417
  55.9 5.2 %copy-start.7 = (bf16[1,128,4096]{2,1,0:T(8,128)(2,1)S(1)}, bf16[1,128,4096]{2,1,0:T(8,128)(2,1)}, u32[]{:S(2)}) copy-start(bf16[1,128,4096]{2,1,0:T(8,128)(2,1)} %text_kv.1) | copy-start | bytes 3145732
  61.0 28.0 %copy-start = (bf16[1,128,2048]{2,1,0:T(8,128)(2,1)S(1)}, bf16[1,128,2048]{2,1,0:T(8,128)(2,1)}, u32[]{:S(2)}) copy-start(bf16[1,128,2048]{2,1,0:T(8,128)(2,1)} %hidden.3) | copy-start | bytes 1572868
  61.0 28.0 %copy-start.1 = (f32[12,3,2048]{2,1,0:T(4,128)S(1)}, f32[12,3,2048]{2,1,0:T(4,128)}, u32[]{:S(2)}) copy-start(f32[12,3,2048]{2,1,0:T(4,128)} %guide_table.1) | copy-start | bytes 884740
  61.1 28.0 %copy-start.2 = (bf16[2048,64]{0,1:T(8,128)(2,1)S(1)}, bf16[2048,64]{0,1:T(8,128)(2,1)}, u32[]{:S(2)}) copy-start(bf16[2048,64]{0,1:T(8,128)(2,1)} %param.18) | copy-start | bytes 786436
  61.1 28.0 %copy-start.3 = (f32[1,3,2048]{2,0,1:T(1,128)S(1)}, f32[1,3,2048]{2,0,1:T(1,128)}, u32[]{:S(2)}) copy-start(f32[1,3,2048]{2,0,1:T(1,128)} %param.16) | copy-start | bytes 73732
  61.1 28.0 %copy-start.4 = (f32[1,64,64]{2,1,0:T(8,128)S(1)}, f32[1,64,64]{2,1,0:T(8,128)}, u32[]{:S(2)}) copy-start(f32[1,64,64]{2,1,0:T(8,128)} %latent.1) | copy-start | bytes 49156
  61.1 28.0 %copy-start.5 = (s32[4]{0:T(128)S(1)}, s32[4]{0:T(128)}, u32[]{:S(2)}) copy-start(s32[4]{0:T(128)} %levels.3) | copy-start | bytes 52
  61.1 28.0 %copy-start.6 = (s32[4]{0:T(128)S(1)}, s32[4]{0:T(128)}, u32[]{:S(2)}) copy-start(s32[4]{0:T(128)} %times.1) | copy-start | bytes 52
  92.4 1.6 %collective-permute-start.2 = (bf16[1024,128]{1,0:T(8,128)(2,1)S(1)}, bf16[1024,128]{1,0:T(8,128)(2,1)S(1)}, u32[]{:S(2)}, u32[]{:S(2)}) collective-permute-start(bf16[1024,128]{1,0:T(8,128)(2,1)S(1)} %get-tuple-element.25), channel_id=1, source_target_pairs={{0,1},{1,0},{2,3},{3,2},{4,5},{5,4},{6,7},{7,6},{8,9},{9,8},{10,11... | collective-permute-start | bytes 786440 | tf_op jit(solution)/shard_map/ppermute | solution.py:451

commit v2 on v1

--- a/solution.py
+++ b/solution.py
@@ -54,21 +54,15 @@
         )
         for index in range(PIECES)
     ]
-    for copy in copies:
-        copy.start()
     far = pl.multiple_of((1 - lax.axis_index("cfg") % 2) * half, half)
     rest = pltpu.make_async_copy(
         hidden.at[0, pl.ds(far, half)], passed.at[pl.ds(0, half)], late.at[0]
     )
+    fetch = pltpu.make_async_copy(modulation, rows_of_mod, late.at[1])
+    for copy in copies:
+        copy.start()
+    fetch.start()
     rest.start()
-    fetch = pltpu.make_async_copy(modulation, rows_of_mod, late.at[1])
-    fetch.start()
-    fetch.wait()
-    mod = jnp.concatenate([rows_of_mod[0], rows_of_mod[1], rows_of_mod[2]], axis=0)
-    high = mod.astype(BF16).astype(F32)
-    zeros = jnp.zeros((5, mod.shape[1]), F32)
-    parts = jnp.concatenate([high, zeros, mod - high, zeros], axis=0)
-    passed[pl.ds(half, 16)] = parts.astype(BF16)
     for index in range(PIECES):
         copies[index].wait()
         span = pl.ds(index * piece, piece)
@@ -76,6 +70,12 @@
             for head in range(heads):
                 column = (kind * heads + head) * HD
                 sent[head, kind, span] = held[span, pl.ds(column, HD)]
+    fetch.wait()
+    mod = jnp.concatenate([rows_of_mod[0], rows_of_mod[1], rows_of_mod[2]], axis=0)
+    high = mod.astype(BF16).astype(F32)
+    zeros = jnp.zeros((5, mod.shape[1]), F32)
+    parts = jnp.concatenate([high, zeros, mod - high, zeros], axis=0)
+    passed[pl.ds(half, 16)] = parts.astype(BF16)
     rest.wait()
 
 

time: 118 us -> 118 us (level)
  no operation moved by 1% of the time
where the time goes in v2:
time: 118 us
  blocking collectives  96.9 us (82%)
  Pallas kernels  17.3 us (15%)
  waiting for transfers between devices  1.53 us (1%)
  between operations  1.45 us (1%)
    all_to_all x1, blocking collectives, local(): lax.all_to_all(sent.reshape(HEADS, 3 * tok_rows, HD), 'seq', split_axis=0...  52.1 us
    all_to_all x1, blocking collectives, local(): lax.all_to_all(terms.reshape(chips, terms.shape[0] // chips, 2 * LATC), (...  22.9 us
    all_to_all x1, blocking collectives, local(): lax.all_to_all(mixed.reshape(members, half_rows, HD), ('cfg', 'seq'), spl...  21.9 us
    pallas_call x1, Pallas kernels, attend_far(): pl.pallas_call(far_kernel, out_shape=(jax.ShapeDtypeStruct((2, sources, r...  5.99 us
    pallas_call x1, Pallas kernels, attend_near(): pl.pallas_call(near_kernel, out_shape=jax.ShapeDtypeStruct((HD + 16, tota...  5.12 us
    pallas_call x1, Pallas kernels, final_layer(): pl.pallas_call(functools.partial(final_kernel, count_scale=count_scale),...  3.29 us
  transfers between devices with their start and end apart: 3, of which 1 were waited for; matrix products, arithmetic and copies ran while one was open for 0% of the time, Pallas kernels for 9%

profile of v2, /device:TPU:2, one launch (start us, length us, event | category | flops | bytes accessed | tf_op | source)
XLA Modules:
  0.0 118.1 jit_solution(17449998267882127783)
XLA Ops:
  0.6 1.6 %shard_map.138 = (bf16[16,3,128,128]{3,2,1,0:T(8,128)(2,1)S(1)}, bf16[80,2048]{1,0:T(8,128)(2,1)S(1)}) custom-call(bf16[1,128,6144]{2,1,0:T(8,128)(2,1)} %packed.1, bf16[1,128,2048]{2,1,0:T(8,128)(2,1)} %hidden.3, f32[3,1,2048]{2,1,0:T(1,128)} %bitcast.16), custom_call_target="tpu_custom_call" | custom-call | tf_op jit(solution)/shard_map/pallas_call | solution.py:89
  2.3 52.1 %all_to_all.15 = bf16[16,384,128]{2,1,0:T(8,128)(2,1)S(1)} all-to-all(bf16[16,384,128]{2,1,0:T(8,128)(2,1)S(1)} %bitcast.12), channel_id=1, replica_groups={{0,2,4,6,8,10,12,14,16,18,20,22,24,26,28,30},{1,3,5,7,9,11,13,15,17,19,..., dimensions={0} | all-to-all | bytes 3145728 | tf_op jit(solution)/shard_map/all_to_all | solution.py:407
  54.4 0.0 collective-permute-start
  54.4 0.7 collective-permute-start.1
  55.8 0.0 copy-start.7
  55.8 5.1 %shard_map.139.state = f32[144,2048]{1,0:T(8,128)S(1)} custom-call(bf16[16,3,128,128]{3,2,1,0:T(8,128)(2,1)S(1)} %bitcast.10), custom_call_target="tpu_custom_call" | custom-call | flops 5368709120 | bytes 4194304 | tf_op jit(solution)/shard_map/pallas_call | solution.py:215
  60.9 0.0 copy-start
  60.9 0.0 copy-start.1
  60.9 0.0 copy-start.2
  60.9 0.0 copy-start.3
  60.9 0.0 copy-start.4
  61.0 0.0 copy-start.5
  61.0 0.0 copy-start.6
  61.0 0.0 collective-permute-done.other
  61.0 6.0 %shard_map.140 = (bf16[2,16,64,128]{3,2,1,0:T(8,128)(2,1)S(1)}, bf16[2048,2048]{1,0:T(8,128)(2,1)S(1)}) custom-call(bf16[16,3,128,128]{3,2,1,0:T(8,128)(2,1)S(1)} %bitcast.11, bf16[16,3,128,128]{3,2,1,0:T(8,128)(2,1)S(1)} %collective-permute-done.other, f32[144,2048]{1,0:T(8,128)S(1)} %shard_map.139.state, bf16[1,128,4096]{2,1,0:T(8,128)(2,1)S(1)} %copy-done.7, ...), custom_call_target="tpu_custom_call" | custom-call | flops 5368709120 | bytes 12582912 | tf_op jit(solution)/shard_map/pallas_call | solution.py:235
  67.0 0.0 collective-permute-done.1.got
  67.0 21.9 %all_to_all.16.heads = bf16[32,64,128]{2,1,0:T(8,128)(2,1)S(1)} all-to-all(bf16[32,64,128]{2,1,0:T(8,128)(2,1)S(1)} %bitcast.14), channel_id=1, replica_groups={{0,2,4,6,8,10,12,14,16,18,20,22,24,26,28,30,32,34,36,38,40,42,44,46,48,..., dimensions={0} | all-to-all | bytes 1048576 | tf_op jit(solution)/shard_map/all_to_all | solution.py:428
  88.9 0.0 copy-done.2
  89.0 3.3 %shard_map.141 = (f32[1,64,64]{2,1,0:T(8,128)}, f32[1,64,64]{2,1,0:T(8,128)}, f32[1024,128]{1,0:T(8,128)S(1)}, bf16[1024,128]{1,0:T(8,128)(2,1)S(1)}) custom-call(s32[4]{0:T(128)S(1)} %copy-done.5, s32[4]{0:T(128)S(1)} %copy-done.6, bf16[32,64,128]{2,1,0:T(8,128)(2,1)S(1)} %all_to_all.16.heads, bf16[2048,2048]{1,0:T(8,128)(2,1)S(1)} %get-tuple-element.20.weight, ...), custom_call_target="tpu_custom_call" | custom-call | flops 1073741824 | bytes 10485760 | tf_op jit(solution)/shard_map/pallas_call | solution.py:337
  92.3 0.1 collective-permute-start.2
  92.4 1.5 %collective-permute-done.2 = bf16[1024,128]{1,0:T(8,128)(2,1)S(1)} collective-permute-done((bf16[1024,128]{1,0:T(8,128)(2,1)S(1)}, bf16[1024,128]{1,0:T(8,128)(2,1)S(1)}, u32[]{:S(2)}, u32[]{:S(2)}) %collective-permute-start.2) | collective-permute-done | bytes 262176 | tf_op jit(solution)/shard_map/ppermute | solution.py:451
  93.9 0.1 fusion
  94.0 22.9 %all_to_all.17 = bf16[128,8,128]{2,1,0:T(8,128)(2,1)S(1)} all-to-all(bf16[128,8,128]{2,1,0:T(8,128)(2,1)S(1)} %fusion), channel_id=1, replica_groups={{0,2,4,6,8,10,12,14,16,18,20,22,24,26,28,30,32,34,36,38,40,42,44,46,48,..., dimensions={0} | all-to-all | bytes 524288 | tf_op jit(solution)/shard_map/all_to_all | solution.py:454
  116.8 1.3 %shard_map.142 = (f32[8,64]{1,0:T(8,128)}, f32[3,8,12]{2,1,0:T(8,128)}) custom-call(s32[4]{0:T(128)S(1)} %copy-done.5, bf16[4,256,128]{2,1,0:T(8,128)(2,1)S(1)} %bitcast.13), custom_call_target="tpu_custom_call" | custom-call | tf_op jit(solution)/shard_map/pallas_call | solution.py:372
  (7 shorter events, 0.0 us)
Async XLA Ops:
  54.4 6.6 %collective-permute-start = (bf16[16,3,128,128]{3,2,1,0:T(8,128)(2,1)S(1)}, bf16[16,3,128,128]{3,2,1,0:T(8,128)(2,1)S(1)}, u32[]{:S(2)}, u32[]{:S(2)}) collective-permute-start(bf16[16,3,128,128]{3,2,1,0:T(8,128)(2,1)S(1)} %bitcast.9), channel_id=1, source_target_pairs={{0,1},{1,0},{2,3},{3,2},{4,5},{5,4},{6,7},{7,6},{8,9},{9,8},{10,11... | collective-permute-start | bytes 4718600 | tf_op jit(solution)/shard_map/ppermute | solution.py:416
  54.4 12.6 %collective-permute-start.1 = (bf16[80,2048]{1,0:T(8,128)(2,1)S(1)}, bf16[80,2048]{1,0:T(8,128)(2,1)S(1)}, u32[]{:S(2)}, u32[]{:S(2)}) collective-permute-start(bf16[80,2048]{1,0:T(8,128)(2,1)S(1)} %get-tuple-element.18), channel_id=1, source_target_pairs={{0,32},{32,0},{64,96},{96,64},{128,160},{160,128},{192,224},{224,1... | collective-permute-start | bytes 983048 | tf_op jit(solution)/shard_map/ppermute | solution.py:417
  55.8 5.2 %copy-start.7 = (bf16[1,128,4096]{2,1,0:T(8,128)(2,1)S(1)}, bf16[1,128,4096]{2,1,0:T(8,128)(2,1)}, u32[]{:S(2)}) copy-start(bf16[1,128,4096]{2,1,0:T(8,128)(2,1)} %text_kv.1) | copy-start | bytes 3145732
  60.9 28.0 %copy-start = (bf16[1,128,2048]{2,1,0:T(8,128)(2,1)S(1)}, bf16[1,128,2048]{2,1,0:T(8,128)(2,1)}, u32[]{:S(2)}) copy-start(bf16[1,128,2048]{2,1,0:T(8,128)(2,1)} %hidden.3) | copy-start | bytes 1572868
  60.9 28.0 %copy-start.1 = (f32[12,3,2048]{2,1,0:T(4,128)S(1)}, f32[12,3,2048]{2,1,0:T(4,128)}, u32[]{:S(2)}) copy-start(f32[12,3,2048]{2,1,0:T(4,128)} %guide_table.1) | copy-start | bytes 884740
  60.9 28.0 %copy-start.2 = (bf16[2048,64]{0,1:T(8,128)(2,1)S(1)}, bf16[2048,64]{0,1:T(8,128)(2,1)}, u32[]{:S(2)}) copy-start(bf16[2048,64]{0,1:T(8,128)(2,1)} %param.18) | copy-start | bytes 786436
  60.9 28.0 %copy-start.3 = (f32[1,3,2048]{2,0,1:T(1,128)S(1)}, f32[1,3,2048]{2,0,1:T(1,128)}, u32[]{:S(2)}) copy-start(f32[1,3,2048]{2,0,1:T(1,128)} %param.16) | copy-start | bytes 73732
  60.9 28.0 %copy-start.4 = (f32[1,64,64]{2,1,0:T(8,128)S(1)}, f32[1,64,64]{2,1,0:T(8,128)}, u32[]{:S(2)}) copy-start(f32[1,64,64]{2,1,0:T(8,128)} %latent.1) | copy-start | bytes 49156
  61.0 28.0 %copy-start.5 = (s32[4]{0:T(128)S(1)}, s32[4]{0:T(128)}, u32[]{:S(2)}) copy-start(s32[4]{0:T(128)} %levels.3) | copy-start | bytes 52
  61.0 28.0 %copy-start.6 = (s32[4]{0:T(128)S(1)}, s32[4]{0:T(128)}, u32[]{:S(2)}) copy-start(s32[4]{0:T(128)} %times.1) | copy-start | bytes 52
  92.3 1.6 %collective-permute-start.2 = (bf16[1024,128]{1,0:T(8,128)(2,1)S(1)}, bf16[1024,128]{1,0:T(8,128)(2,1)S(1)}, u32[]{:S(2)}, u32[]{:S(2)}) collective-permute-start(bf16[1024,128]{1,0:T(8,128)(2,1)S(1)} %get-tuple-element.25), channel_id=1, source_target_pairs={{0,1},{1,0},{2,3},{3,2},{4,5},{5,4},{6,7},{7,6},{8,9},{9,8},{10,11... | collective-permute-start | bytes 786440 | tf_op jit(solution)/shard_map/ppermute | solution.py:451

commit v3 on v1

--- a/solution.py
+++ b/solution.py
@@ -54,15 +54,15 @@
         )
         for index in range(PIECES)
     ]
-    for copy in copies:
-        copy.start()
     far = pl.multiple_of((1 - lax.axis_index("cfg") % 2) * half, half)
     rest = pltpu.make_async_copy(
         hidden.at[0, pl.ds(far, half)], passed.at[pl.ds(0, half)], late.at[0]
     )
-    rest.start()
     fetch = pltpu.make_async_copy(modulation, rows_of_mod, late.at[1])
     fetch.start()
+    for copy in copies:
+        copy.start()
+    rest.start()
     fetch.wait()
     mod = jnp.concatenate([rows_of_mod[0], rows_of_mod[1], rows_of_mod[2]], axis=0)
     high = mod.astype(BF16).astype(F32)

time: 118 us -> 118 us (level)
  no operation moved by 1% of the time
where the time goes in v3:
time: 118 us
  blocking collectives  96.9 us (82%)
  Pallas kernels  17.3 us (15%)
  waiting for transfers between devices  1.53 us (1%)
  between operations  1.45 us (1%)
    all_to_all x1, blocking collectives, local(): lax.all_to_all(sent.reshape(HEADS, 3 * tok_rows, HD), 'seq', split_axis=0...  52.1 us
    all_to_all x1, blocking collectives, local(): lax.all_to_all(terms.reshape(chips, terms.shape[0] // chips, 2 * LATC), (...  22.9 us
    all_to_all x1, blocking collectives, local(): lax.all_to_all(mixed.reshape(members, half_rows, HD), ('cfg', 'seq'), spl...  21.9 us
    pallas_call x1, Pallas kernels, attend_far(): pl.pallas_call(far_kernel, out_shape=(jax.ShapeDtypeStruct((2, sources, r...  5.99 us
    pallas_call x1, Pallas kernels, attend_near(): pl.pallas_call(near_kernel, out_shape=jax.ShapeDtypeStruct((HD + 16, tota...  5.12 us
    pallas_call x1, Pallas kernels, final_layer(): pl.pallas_call(functools.partial(final_kernel, count_scale=count_scale),...  3.29 us
  transfers between devices with their start and end apart: 3, of which 1 were waited for; matrix products, arithmetic and copies ran while one was open for 0% of the time, Pallas kernels for 9%

profile of v3, /device:TPU:2, one launch (start us, length us, event | category | flops | bytes accessed | tf_op | source)
XLA Modules:
  0.0 118.1 jit_solution(6616503289604003129)
XLA Ops:
  0.6 1.6 %shard_map.138 = (bf16[16,3,128,128]{3,2,1,0:T(8,128)(2,1)S(1)}, bf16[80,2048]{1,0:T(8,128)(2,1)S(1)}) custom-call(bf16[1,128,6144]{2,1,0:T(8,128)(2,1)} %packed.1, bf16[1,128,2048]{2,1,0:T(8,128)(2,1)} %hidden.3, f32[3,1,2048]{2,1,0:T(1,128)} %bitcast.16), custom_call_target="tpu_custom_call" | custom-call | tf_op jit(solution)/shard_map/pallas_call | solution.py:89
  2.3 52.1 %all_to_all.15 = bf16[16,384,128]{2,1,0:T(8,128)(2,1)S(1)} all-to-all(bf16[16,384,128]{2,1,0:T(8,128)(2,1)S(1)} %bitcast.12), channel_id=1, replica_groups={{0,2,4,6,8,10,12,14,16,18,20,22,24,26,28,30},{1,3,5,7,9,11,13,15,17,19,..., dimensions={0} | all-to-all | bytes 3145728 | tf_op jit(solution)/shard_map/all_to_all | solution.py:407
  54.4 0.0 collective-permute-start
  54.4 0.7 collective-permute-start.1
  55.8 0.0 copy-start.7
  55.8 5.1 %shard_map.139.state = f32[144,2048]{1,0:T(8,128)S(1)} custom-call(bf16[16,3,128,128]{3,2,1,0:T(8,128)(2,1)S(1)} %bitcast.10), custom_call_target="tpu_custom_call" | custom-call | flops 5368709120 | bytes 4194304 | tf_op jit(solution)/shard_map/pallas_call | solution.py:215
  60.9 0.0 copy-start
  60.9 0.0 copy-start.1
  60.9 0.0 copy-start.2
  60.9 0.0 copy-start.3
  60.9 0.0 copy-start.4
  61.0 0.0 copy-start.5
  61.0 0.0 copy-start.6
  61.0 0.0 collective-permute-done.other
  61.0 6.0 %shard_map.140 = (bf16[2,16,64,128]{3,2,1,0:T(8,128)(2,1)S(1)}, bf16[2048,2048]{1,0:T(8,128)(2,1)S(1)}) custom-call(bf16[16,3,128,128]{3,2,1,0:T(8,128)(2,1)S(1)} %bitcast.11, bf16[16,3,128,128]{3,2,1,0:T(8,128)(2,1)S(1)} %collective-permute-done.other, f32[144,2048]{1,0:T(8,128)S(1)} %shard_map.139.state, bf16[1,128,4096]{2,1,0:T(8,128)(2,1)S(1)} %copy-done.7, ...), custom_call_target="tpu_custom_call" | custom-call | flops 5368709120 | bytes 12582912 | tf_op jit(solution)/shard_map/pallas_call | solution.py:235
  67.0 0.0 collective-permute-done.1.got
  67.0 21.9 %all_to_all.16.heads = bf16[32,64,128]{2,1,0:T(8,128)(2,1)S(1)} all-to-all(bf16[32,64,128]{2,1,0:T(8,128)(2,1)S(1)} %bitcast.14), channel_id=1, replica_groups={{0,2,4,6,8,10,12,14,16,18,20,22,24,26,28,30,32,34,36,38,40,42,44,46,48,..., dimensions={0} | all-to-all | bytes 1048576 | tf_op jit(solution)/shard_map/all_to_all | solution.py:428
  88.9 0.0 copy-done.2
  89.0 3.3 %shard_map.141 = (f32[1,64,64]{2,1,0:T(8,128)}, f32[1,64,64]{2,1,0:T(8,128)}, f32[1024,128]{1,0:T(8,128)S(1)}, bf16[1024,128]{1,0:T(8,128)(2,1)S(1)}) custom-call(s32[4]{0:T(128)S(1)} %copy-done.5, s32[4]{0:T(128)S(1)} %copy-done.6, bf16[32,64,128]{2,1,0:T(8,128)(2,1)S(1)} %all_to_all.16.heads, bf16[2048,2048]{1,0:T(8,128)(2,1)S(1)} %get-tuple-element.20.weight, ...), custom_call_target="tpu_custom_call" | custom-call | flops 1073741824 | bytes 10485760 | tf_op jit(solution)/shard_map/pallas_call | solution.py:337
  92.3 0.1 collective-permute-start.2
  92.4 1.5 %collective-permute-done.2 = bf16[1024,128]{1,0:T(8,128)(2,1)S(1)} collective-permute-done((bf16[1024,128]{1,0:T(8,128)(2,1)S(1)}, bf16[1024,128]{1,0:T(8,128)(2,1)S(1)}, u32[]{:S(2)}, u32[]{:S(2)}) %collective-permute-start.2) | collective-permute-done | bytes 262176 | tf_op jit(solution)/shard_map/ppermute | solution.py:451
  93.9 0.1 fusion
  94.0 22.9 %all_to_all.17 = bf16[128,8,128]{2,1,0:T(8,128)(2,1)S(1)} all-to-all(bf16[128,8,128]{2,1,0:T(8,128)(2,1)S(1)} %fusion), channel_id=1, replica_groups={{0,2,4,6,8,10,12,14,16,18,20,22,24,26,28,30,32,34,36,38,40,42,44,46,48,..., dimensions={0} | all-to-all | bytes 524288 | tf_op jit(solution)/shard_map/all_to_all | solution.py:454
  116.8 1.3 %shard_map.142 = (f32[8,64]{1,0:T(8,128)}, f32[3,8,12]{2,1,0:T(8,128)}) custom-call(s32[4]{0:T(128)S(1)} %copy-done.5, bf16[4,256,128]{2,1,0:T(8,128)(2,1)S(1)} %bitcast.13), custom_call_target="tpu_custom_call" | custom-call | tf_op jit(solution)/shard_map/pallas_call | solution.py:372
  (7 shorter events, 0.0 us)
Async XLA Ops:
  54.4 6.6 %collective-permute-start = (bf16[16,3,128,128]{3,2,1,0:T(8,128)(2,1)S(1)}, bf16[16,3,128,128]{3,2,1,0:T(8,128)(2,1)S(1)}, u32[]{:S(2)}, u32[]{:S(2)}) collective-permute-start(bf16[16,3,128,128]{3,2,1,0:T(8,128)(2,1)S(1)} %bitcast.9), channel_id=1, source_target_pairs={{0,1},{1,0},{2,3},{3,2},{4,5},{5,4},{6,7},{7,6},{8,9},{9,8},{10,11... | collective-permute-start | bytes 4718600 | tf_op jit(solution)/shard_map/ppermute | solution.py:416
  54.4 12.6 %collective-permute-start.1 = (bf16[80,2048]{1,0:T(8,128)(2,1)S(1)}, bf16[80,2048]{1,0:T(8,128)(2,1)S(1)}, u32[]{:S(2)}, u32[]{:S(2)}) collective-permute-start(bf16[80,2048]{1,0:T(8,128)(2,1)S(1)} %get-tuple-element.18), channel_id=1, source_target_pairs={{0,32},{32,0},{64,96},{96,64},{128,160},{160,128},{192,224},{224,1... | collective-permute-start | bytes 983048 | tf_op jit(solution)/shard_map/ppermute | solution.py:417
  55.8 5.2 %copy-start.7 = (bf16[1,128,4096]{2,1,0:T(8,128)(2,1)S(1)}, bf16[1,128,4096]{2,1,0:T(8,128)(2,1)}, u32[]{:S(2)}) copy-start(bf16[1,128,4096]{2,1,0:T(8,128)(2,1)} %text_kv.1) | copy-start | bytes 3145732
  60.9 28.0 %copy-start = (bf16[1,128,2048]{2,1,0:T(8,128)(2,1)S(1)}, bf16[1,128,2048]{2,1,0:T(8,128)(2,1)}, u32[]{:S(2)}) copy-start(bf16[1,128,2048]{2,1,0:T(8,128)(2,1)} %hidden.3) | copy-start | bytes 1572868
  60.9 28.0 %copy-start.1 = (f32[12,3,2048]{2,1,0:T(4,128)S(1)}, f32[12,3,2048]{2,1,0:T(4,128)}, u32[]{:S(2)}) copy-start(f32[12,3,2048]{2,1,0:T(4,128)} %guide_table.1) | copy-start | bytes 884740
  60.9 28.0 %copy-start.2 = (bf16[2048,64]{0,1:T(8,128)(2,1)S(1)}, bf16[2048,64]{0,1:T(8,128)(2,1)}, u32[]{:S(2)}) copy-start(bf16[2048,64]{0,1:T(8,128)(2,1)} %param.18) | copy-start | bytes 786436
  60.9 28.0 %copy-start.3 = (f32[1,3,2048]{2,0,1:T(1,128)S(1)}, f32[1,3,2048]{2,0,1:T(1,128)}, u32[]{:S(2)}) copy-start(f32[1,3,2048]{2,0,1:T(1,128)} %param.16) | copy-start | bytes 73732
  60.9 28.0 %copy-start.4 = (f32[1,64,64]{2,1,0:T(8,128)S(1)}, f32[1,64,64]{2,1,0:T(8,128)}, u32[]{:S(2)}) copy-start(f32[1,64,64]{2,1,0:T(8,128)} %latent.1) | copy-start | bytes 49156
  61.0 28.0 %copy-start.5 = (s32[4]{0:T(128)S(1)}, s32[4]{0:T(128)}, u32[]{:S(2)}) copy-start(s32[4]{0:T(128)} %levels.3) | copy-start | bytes 52
  61.0 28.0 %copy-start.6 = (s32[4]{0:T(128)S(1)}, s32[4]{0:T(128)}, u32[]{:S(2)}) copy-start(s32[4]{0:T(128)} %times.1) | copy-start | bytes 52
  92.3 1.6 %collective-permute-start.2 = (bf16[1024,128]{1,0:T(8,128)(2,1)S(1)}, bf16[1024,128]{1,0:T(8,128)(2,1)S(1)}, u32[]{:S(2)}, u32[]{:S(2)}) collective-permute-start(bf16[1024,128]{1,0:T(8,128)(2,1)S(1)} %get-tuple-element.25), channel_id=1, source_target_pairs={{0,1},{1,0},{2,3},{3,2},{4,5},{5,4},{6,7},{7,6},{8,9},{9,8},{10,11... | collective-permute-start | bytes 786440 | tf_op jit(solution)/shard_map/ppermute | solution.py:451
